TPU v7x, 256 devices: a whole 4x4x8 slice. The times are simulated.
256 devices in a mesh: dp: 4 (over y), gx: 4 (over x), gy: 16 (over z, core).
Axes of the slice: x: 4, y: 4, z: 8, core: 2. Of those that a mesh axis runs over, the one named last changes fastest.
Arguments:
- field: bfloat16 [4, 64, 32, 20, 2048], P('dp', 'gx', 'gy'), may hold values from -6 to 6
- cotangent: bfloat16 [4, 64, 32, 20, 2048], P('dp', 'gx', 'gy'), may hold values from -6 to 6
- spectral_weight: bfloat16 [24, 24, 20, 20, 192], P(None, None, None, None, ('gx', 'gy')), may hold values from -2.5 to 2.5
- bypass_weight: bfloat16 [20, 20], replicated, may hold values from -1.25 to 1.25
Outputs:
- grad_field: bfloat16 [4, 64, 32, 20, 2048], P('dp', 'gx', 'gy')
- grad_spectral: float32 [24, 24, 20, 20, 192], P(None, None, None, None, ('gx', 'gy'))
- grad_bypass: float32 [20, 20], replicated
All inputs are finite; a program needn't handle non-finite values.
Results may differ from a plain program's by a relative error of at most 0.034.
Values may be sent and summed in bfloat16 or wider, within the bound.
No kernel may reach another device: no remote copies, remote signals or barrier semaphores. Data moves between devices by JAX's collectives and lax.ppermute only.
A program may use at most 192 MiB of HBM per device.

v0:
```python
import math
import jax
import jax.numpy as jnp
from jax import lax
from jax.sharding import PartitionSpec as P

MX = 12
MY = 12
MZ = 12
MT = 4
NZ = 128
NT = 16


def basis(length, kept):
    places = lax.iota(jnp.int32, length)
    orders = lax.iota(jnp.int32, kept)
    cos_arg = places[:, None] * orders[None, :] % length
    sin_arg = places[:, None] * (orders[None, :] + 1) % length
    step_angle = 2.0 * math.pi / length
    scale = math.sqrt(2.0 / length)
    cos_part = jnp.cos(cos_arg.astype(jnp.float32) * step_angle)
    sin_part = jnp.sin(sin_arg.astype(jnp.float32) * step_angle)
    return jnp.concatenate([cos_part, sin_part], axis=1) * scale


def mode_dot(form, data, table):
    upper = table.astype(jnp.bfloat16)
    lower = (table - upper.astype(jnp.float32)).astype(jnp.bfloat16)
    first = jnp.einsum(form, data, upper, preferred_element_type=jnp.float32)
    return first + jnp.einsum(form, data, lower, preferred_element_type=jnp.float32)


def body(field, cotangent, spectral_weight, bypass_weight):
    cells_x = field.shape[1]
    cells_y = field.shape[2]
    channels = field.shape[3]
    parts_x = lax.axis_size("gx")
    parts_y = lax.axis_size("gy")
    table_x = basis(cells_x * parts_x, MX)
    table_y = basis(cells_y * parts_y, MY)
    table_z = basis(NZ, MZ)
    table_t = basis(NT, MT)
    modes_zt = 4 * MZ * MT
    table_zt = (table_z[:, None, :, None] * table_t[None, :, None, :]).reshape(NZ * NT, modes_zt)

    def analyze(cells):
        matrix = cells.reshape(-1, NZ * NT)
        coeff = mode_dot("rp,pq->rq", matrix, table_zt).astype(jnp.bfloat16)
        coeff = coeff.reshape(cells_x, cells_y, channels, modes_zt)
        along_x = lax.all_to_all(coeff, "gx", split_axis=3, concat_axis=0, tiled=True)
        partial_x = mode_dot("xycq,xk->kycq", along_x, table_x).astype(jnp.bfloat16)
        along_y = lax.all_to_all(partial_x, "gy", split_axis=3, concat_axis=1, tiled=True)
        return mode_dot("kycq,yl->klcq", along_y, table_y).astype(jnp.bfloat16)

    def synthesize(spectrum):
        partial_y = mode_dot("klcq,yl->kycq", spectrum, table_y).astype(jnp.bfloat16)
        returned = lax.all_to_all(partial_y, "gy", split_axis=1, concat_axis=3, tiled=True)
        partial_x = mode_dot("kycq,xk->xycq", returned, table_x).astype(jnp.bfloat16)
        coeff = lax.all_to_all(partial_x, "gx", split_axis=0, concat_axis=3, tiled=True)
        matrix = coeff.reshape(-1, modes_zt)
        values = mode_dot("rq,pq->rp", matrix, table_zt)
        return values.reshape(1, cells_x, cells_y, channels, NZ * NT)

    spectrum = analyze(field)
    mixed = jnp.einsum(
        "klcq,klcoq->kloq", spectrum, spectral_weight, preferred_element_type=jnp.float32
    ).astype(jnp.bfloat16)
    spatial = synthesize(mixed)
    bypass = jnp.einsum("bxyip,io->bxyop", field, bypass_weight, preferred_element_type=jnp.float32)
    pre = spatial + bypass
    unused, pullback = jax.vjp(jax.nn.gelu, pre)
    (slope,) = pullback(cotangent.astype(jnp.float32))
    upstream = slope.astype(jnp.bfloat16)
    bypass_term = jnp.einsum("bxyip,bxyop->io", field, upstream, preferred_element_type=jnp.float32)
    grad_bypass = lax.psum(bypass_term, ("dp", "gx", "gy"))
    spectrum_up = analyze(upstream)
    local_grad = jnp.einsum(
        "klcq,kloq->klcoq", spectrum, spectrum_up, preferred_element_type=jnp.float32
    )
    grad_spectral = lax.psum(local_grad.astype(jnp.bfloat16), "dp").astype(jnp.float32)
    spectrum_back = jnp.einsum(
        "kloq,klcoq->klcq", spectrum_up, spectral_weight, preferred_element_type=jnp.float32
    ).astype(jnp.bfloat16)
    through_bypass = jnp.einsum(
        "bxyop,io->bxyip", upstream, bypass_weight, preferred_element_type=jnp.float32
    )
    grad_field = (synthesize(spectrum_back) + through_bypass).astype(jnp.bfloat16)
    return (grad_field, grad_spectral, grad_bypass)


def solution(mesh):
    in_specs = (
        P("dp", "gx", "gy", None, None),
        P("dp", "gx", "gy", None, None),
        P(None, None, None, None, ("gx", "gy")),
        P(),
    )
    out_specs = (P("dp", "gx", "gy", None, None), P(None, None, None, None, ("gx", "gy")), P())
    return jax.shard_map(body, mesh=mesh, in_specs=in_specs, out_specs=out_specs, check_vma=False)
```

profile of v0, /device:TPU:1, one launch (start us, length us, event | category | flops | bytes accessed | tf_op | source)
XLA Modules:
  0.0 493.5 jit_solution(16601009664940160456)
XLA Ops:
  7.5 4.7 copy.145
  15.8 6.2 %fusion = (bf16[128,16,24,8]{1,0,3,2:T(8,128)(2,1)}, bf16[128,16,24,8]{1,0,3,2:T(8,128)(2,1)}) fusion(f32[16,8]{0,1:T(8,128)S(1)} %maximum_multiply_fusion.3, f32[128,24]{0,1:T(8,128)S(1)} %maximum_multiply_fusion.2), kind=kLoop, calls=%fused_computation.5 | loop fusion | flops 1966080 | bytes 1585664 | tf_op jit(solution)/shard_map/convert_element_type | solution.py:29
  22.0 11.6 %convert_element_type.256 = bf16[2048,192]{0,1:T(8,128)(2,1)S(1)} reshape(bf16[128,16,24,8]{1,0,3,2:T(8,128)(2,1)} %get-tuple-element.26) | data formatting | bytes 1572864 | tf_op jit(solution)/shard_map/convert_element_type | solution.py:29
  33.7 12.3 %convert_element_type.253 = bf16[2048,192]{0,1:T(8,128)(2,1)} reshape(bf16[128,16,24,8]{1,0,3,2:T(8,128)(2,1)} %get-tuple-element.27) | data formatting | bytes 1572864 | tf_op jit(solution)/shard_map/convert_element_type | solution.py:28
  49.9 5.9 %reshape.160 = bf16[16,2,20,192]{2,1,0,3:T(2,128)(2,1)S(1)} reshape(bf16[640,192]{0,1:T(8,128)(2,1)} %fusion.30) | data formatting | bytes 491520 | tf_op jit(solution)/shard_map/reshape | solution.py:50
  55.9 4.2 reshape.162
  60.0 4.8 all-to-all-start
  65.0 5.3 %all-to-all-done = bf16[4,2,15360]{2,1,0:T(2,128)(2,1)S(1)} async-done(((bf16[4,2,15360]{2,1,0:T(2,128)(2,1)}), bf16[4,2,15360]{2,1,0:T(2,128)(2,1)S(1)}, u32[]{:S(2)}, u32[]{:S(2)}) %all-to-all-start) | async-done | bytes 245792 | tf_op jit(solution)/shard_map/all_to_all | solution.py:51
  70.3 4.1 reshape.163
  79.3 10.9 %all-to-all-start.1 = ((bf16[16,2,1440]{2,1,0:T(2,128)(2,1)}), bf16[16,2,1440]{2,1,0:T(2,128)(2,1)S(1)}, u32[]{:S(2)}, u32[]{:S(2)}) async-start(bf16[16,2,1440]{2,1,0:T(2,128)(2,1)} %reshape.164), calls=%async_computation.1 | async-start | bytes 196608 | tf_op jit(solution)/shard_map/all_to_all | solution.py:53
  90.4 8.2 %all-to-all-done.1 = bf16[16,2,1440]{2,1,0:T(2,128)(2,1)S(1)} async-done(((bf16[16,2,1440]{2,1,0:T(2,128)(2,1)}), bf16[16,2,1440]{2,1,0:T(2,128)(2,1)S(1)}, u32[]{:S(2)}, u32[]{:S(2)}) %all-to-all-start.1) | async-done | bytes 92192 | tf_op jit(solution)/shard_map/all_to_all | solution.py:53
  101.2 5.0 %multiply_reduce_fusion.1 = bf16[24,24,3,20]{1,0,2,3:T(8,128)(2,1)S(1)} fusion(f32[24,24,3,20]{1,0,2,3:T(8,128)S(1)} %copy.223, bf16[24,24,20,20,3]{1,0,4,3,2:T(8,128)(2,1)} %param.6), kind=kLoop, calls=%fused_computation.3 | loop fusion | flops 2039040 | bytes 1589760 | tf_op jit(solution)/shard_map/klcq,klcoq->kloq/dot_general | solution.py:66
  107.7 10.9 %all_to_all.138 = bf16[16,2,1440]{2,1,0:T(2,128)(2,1)S(1)} all-to-all(bf16[16,2,1440]{2,1,0:T(2,128)(2,1)S(1)} %reshape.166), channel_id=1, replica_groups=mesh['dp'=4,'gx'=4,'gy'=16] {'gy'}, dimensions={0} | all-to-all | bytes 184320 | tf_op jit(solution)/shard_map/all_to_all | solution.py:58
  122.3 9.6 %all_to_all.139 = bf16[4,2,15360]{2,1,0:T(2,128)(2,1)S(1)} all-to-all(bf16[4,2,15360]{2,1,0:T(2,128)(2,1)S(1)} %reshape.168), channel_id=1, replica_groups=mesh['dp'=4,'gx'=4,'gy'=16] {'gx'}, dimensions={0} | all-to-all | bytes 491520 | tf_op jit(solution)/shard_map/all_to_all | solution.py:60
  139.5 6.7 %reshape.142 = f32[1,16,2,20,2048]{4,3,2,1,0:T(8,128)} reshape(f32[640,2048]{1,0:T(8,128)} %convolution_add_fusion.1) | data formatting | bytes 10485760 | tf_op jit(solution)/shard_map/reshape | solution.py:63
  146.1 11.0 %fusion.4 = bf16[1,16,2,20,2048]{4,3,2,1,0:T(8,128)(2,1)} fusion(f32[1,16,2,20,2048]{4,3,2,1,0:T(8,128)} %reshape.142, bf16[1,16,2,20,2048]{4,2,3,1,0:T(2,128)(2,1)} %param.5, bf16[16,2,20,2048]{3,1,2,0:T(2,128)(2,1)} %bitcast.208, bf16[20,20]{1,0:T(8,128)(2,1)S(1)} %copy-done), kind=kOutput, calls=%fused_computation.13 | convolution fusion | flops 81264640 | bytes 13108000 | tf_op jit(solution)/shard_map/bxyip,io->bxyop/dot_general | solution.py:70
  157.1 5.3 %reshape.144 = bf16[640,2048]{1,0:T(8,128)(2,1)} reshape(bf16[1,16,2,20,2048]{4,3,2,1,0:T(8,128)(2,1)} %fusion.4) | data formatting | bytes 5242880 | tf_op jit(solution)/shard_map/reshape | solution.py:48
  168.0 3.8 reshape.161
  175.3 8.8 %all_to_all.140 = bf16[4,2,15360]{2,1,0:T(2,128)(2,1)} all-to-all(bf16[4,2,15360]{2,1,0:T(2,128)(2,1)S(1)} %reshape.170), channel_id=1, replica_groups=mesh['dp'=4,'gx'=4,'gy'=16] {'gx'}, dimensions={0} | all-to-all | bytes 491520 | tf_op jit(solution)/shard_map/all_to_all | solution.py:51
  184.2 6.0 %reshape.171 = bf16[192,16,2,20]{3,2,1,0:T(2,128)(2,1)S(1)} reshape(bf16[4,2,15360]{2,1,0:T(2,128)(2,1)} %all_to_all.140) | data formatting | bytes 491520
  196.9 5.2 %all-to-all-start.5 = ((bf16[16,2,1440]{2,1,0:T(2,128)(2,1)}), bf16[16,2,1440]{2,1,0:T(2,128)(2,1)S(1)}, u32[]{:S(2)}, u32[]{:S(2)}) async-start(bf16[16,2,1440]{2,1,0:T(2,128)(2,1)} %reshape.172), calls=%async_computation.5 | async-start | bytes 196608 | tf_op jit(solution)/shard_map/all_to_all | solution.py:53
  204.3 6.3 %all-to-all-done.5 = bf16[16,2,1440]{2,1,0:T(2,128)(2,1)S(1)} async-done(((bf16[16,2,1440]{2,1,0:T(2,128)(2,1)}), bf16[16,2,1440]{2,1,0:T(2,128)(2,1)S(1)}, u32[]{:S(2)}, u32[]{:S(2)}) %all-to-all-start.5) | async-done | bytes 92192 | tf_op jit(solution)/shard_map/all_to_all | solution.py:53
  214.5 5.0 %multiply_reduce_fusion = bf16[24,24,3,20]{1,0,2,3:T(8,128)(2,1)S(1)} fusion(f32[24,24,3,20]{1,0,2,3:T(8,128)S(1)} %copy.224, bf16[24,24,20,20,3]{1,0,4,3,2:T(8,128)(2,1)} %param.6), kind=kLoop, calls=%fused_computation.2 | loop fusion | flops 2039040 | bytes 1589760 | tf_op jit(solution)/shard_map/kloq,klcoq->klcq/dot_general | solution.py:82
  221.6 3.7 all-to-all-start.6
  225.3 4.9 fusion.31
  230.2 76.2 %psum.15 = f32[20,20]{0,1:T(8,128)S(1)} all-reduce(f32[20,20]{0,1:T(8,128)S(1)} %fusion.31), channel_id=1, replica_groups=mesh['dp'=4,'gx'=4,'gy'=16] {'dp','gx','gy'}, use_global_device_ids=true, to_apply=%region_1.2 | all-reduce | flops 400 | bytes 3200 | tf_op jit(solution)/shard_map/psum | solution.py:76
  321.4 5.3 %fusion.1 = bf16[24,24,20,20,3]{1,0,4,3,2:T(8,128)(2,1)} fusion(f32[24,24,3,20]{1,0,2,3:T(8,128)S(1)} %copy-done.3, f32[24,24,3,20]{1,0,2,3:T(8,128)} %copy.186), kind=kLoop, calls=%fused_computation.10 | loop fusion | flops 1382400 | bytes 1658880 | tf_op jit(solution)/shard_map/convert_element_type | solution.py:81
  334.4 7.2 %reshape.147 = f32[1,16,2,20,2048]{4,3,2,1,0:T(8,128)} reshape(f32[640,2048]{1,0:T(8,128)} %convolution_add_fusion) | data formatting | bytes 10485760 | tf_op jit(solution)/shard_map/reshape | solution.py:63
  341.6 4.1 fusion.12
  345.7 4.2 copy.189
  349.9 126.0 %all-reduce.2.cloned.1.call-done = bf16[24,24,20,20,3]{1,0,4,3,2:T(8,128)(2,1)} async-done(((bf16[24,24,20,20,3]{1,0,4,3,2:T(8,128)(2,1)}), bf16[24,24,20,20,3]{1,0,4,3,2:T(8,128)(2,1)}) %all-reduce.2.cloned.1.call-update) | async-done | bytes 1382416 | tf_op jit(solution)/shard_map/psum | solution.py:81
  475.9 10.2 %convert_element_type.284 = f32[24,24,20,20,3]{1,0,4,3,2:T(8,128)} convert(bf16[24,24,20,20,3]{1,0,4,3,2:T(8,128)(2,1)} %all-reduce.2.cloned.1.call-done) | non-fusion elementwise | flops 691200 | bytes 4147200 | tf_op jit(solution)/shard_map/convert_element_type | solution.py:81
  (90 shorter events, 74.8 us)
Async XLA Ops:
  7.2 139.0 %copy-start = (bf16[20,20]{1,0:T(8,128)(2,1)S(1)}, bf16[20,20]{1,0:T(8,128)(2,1)}, u32[]{:S(2)}) copy-start(bf16[20,20]{1,0:T(8,128)(2,1)} %param.7) | copy-start | bytes 2404
  60.0 10.3 %all-to-all-start = ((bf16[4,2,15360]{2,1,0:T(2,128)(2,1)}), bf16[4,2,15360]{2,1,0:T(2,128)(2,1)S(1)}, u32[]{:S(2)}, u32[]{:S(2)}) async-start(bf16[4,2,15360]{2,1,0:T(2,128)(2,1)} %reshape.162), calls=%async_computation | async-start | bytes 491520 | tf_op jit(solution)/shard_map/all_to_all | solution.py:51
  79.3 19.3 %all-to-all-start.1 = ((bf16[16,2,1440]{2,1,0:T(2,128)(2,1)}), bf16[16,2,1440]{2,1,0:T(2,128)(2,1)S(1)}, u32[]{:S(2)}, u32[]{:S(2)}) async-start(bf16[16,2,1440]{2,1,0:T(2,128)(2,1)} %reshape.164), calls=%async_computation.1 | async-start | bytes 196608 | tf_op jit(solution)/shard_map/all_to_all | solution.py:53
  119.1 16.2 %copy-start.1 = (bf16[2048,192]{0,1:T(8,128)(2,1)S(1)}, bf16[2048,192]{0,1:T(8,128)(2,1)}, u32[]{:S(2)}) copy-start(bf16[2048,192]{0,1:T(8,128)(2,1)} %convert_element_type.253) | copy-start | bytes 2359300
  196.9 13.7 %all-to-all-start.5 = ((bf16[16,2,1440]{2,1,0:T(2,128)(2,1)}), bf16[16,2,1440]{2,1,0:T(2,128)(2,1)S(1)}, u32[]{:S(2)}, u32[]{:S(2)}) async-start(bf16[16,2,1440]{2,1,0:T(2,128)(2,1)} %reshape.172), calls=%async_computation.5 | async-start | bytes 196608 | tf_op jit(solution)/shard_map/all_to_all | solution.py:53
  221.6 87.7 %all-to-all-start.6 = ((bf16[16,2,1440]{2,1,0:T(2,128)(2,1)}), bf16[16,2,1440]{2,1,0:T(2,128)(2,1)S(1)}, u32[]{:S(2)}, u32[]{:S(2)}) async-start(bf16[16,2,1440]{2,1,0:T(2,128)(2,1)} %reshape.174), calls=%async_computation.6 | async-start | bytes 196608 | tf_op jit(solution)/shard_map/all_to_all | solution.py:58
  230.2 91.2 %copy-start.3 = (f32[24,24,3,20]{1,0,2,3:T(8,128)S(1)}, f32[24,24,3,20]{1,0,2,3:T(8,128)}, u32[]{:S(2)}) copy-start(f32[24,24,3,20]{1,0,2,3:T(8,128)} %copy.187) | copy-start | bytes 414724
  317.9 9.0 %all-to-all-start.7 = ((bf16[4,2,15360]{2,1,0:T(2,128)(2,1)}), bf16[4,2,15360]{2,1,0:T(2,128)(2,1)S(1)}, u32[]{:S(2)}, u32[]{:S(2)}) async-start(bf16[4,2,15360]{2,1,0:T(2,128)(2,1)} %reshape.176), calls=%async_computation.7 | async-start | bytes 491520 | tf_op jit(solution)/shard_map/all_to_all | solution.py:60
  321.3 154.6 %all-reduce.2.cloned.1.call-start = ((), (), s32[]{:S(2)}) async-start(), calls=%async_computation.8 | async-start | bytes 14745600 | tf_op jit(solution)/shard_map/psum | solution.py:81
  334.4 7.2 %copy-start.2 = (bf16[1,16,2,20,2048]{4,3,2,1,0:T(8,128)(2,1)S(1)}, bf16[1,16,2,20,2048]{4,3,2,1,0:T(8,128)(2,1)}, u32[]{:S(2)}) copy-start(bf16[1,16,2,20,2048]{4,3,2,1,0:T(8,128)(2,1)} %fusion.4) | copy-start | bytes 7864324
Sparse Core Ops, SparseCore 0:
  326.8 149.0 all-reduce.1
where the time goes:
time: 503 us; the launch traced here: 493 us
  waiting for transfers between devices  146 us (29%)
  local copies, waits for them, and re-layouts  120 us (24%)
  blocking collectives  105 us (21%)
  matrix products  46.5 us (9%)
  other arithmetic  32.3 us (6%)
  starting transfers between devices  28 us (6%)
  between operations  15.1 us (3%)
    psum x1, waiting for transfers between devices, body(): lax.psum(local_grad.astype(jnp.bfloat16), 'dp').astype(jnp.float32)  126 us
    psum x1, blocking collectives, body(): grad_bypass = lax.psum(bypass_term, ('dp', 'gx', 'gy'))  76.2 us
    unnamed x29, local copies, waits for them, and re-layouts  39.6 us
    dot_general x12, matrix products, mode_dot(): jnp.einsum(form, data, lower, preferred_element_type=jnp.float32)  16.9 us
    all_to_all x2, starting transfers between devices, analyze(): lax.all_to_all(partial_x, 'gy', split_axis=3, concat_axis=1, tiled=True)  16.1 us
    all_to_all x2, waiting for transfers between devices, analyze(): lax.all_to_all(partial_x, 'gy', split_axis=3, concat_axis=1, tiled=True)  14.5 us
    reshape x2, local copies, waits for them, and re-layouts, synthesize(): return values.reshape(1, cells_x, cells_y, channels, NZ * NT)  13.9 us
    convert_element_type x1, local copies, waits for them, and re-layouts, mode_dot(): upper = table.astype(jnp.bfloat16)  12.3 us
  transfers between devices with their start and end apart: 6, of which 5 were waited for; matrix products, arithmetic and copies ran while one was open for 8% of the time, Pallas kernels for 0%

commit v1 on v0

--- a/solution.py
+++ b/solution.py
@@ -10,6 +10,17 @@
 MT = 4
 NZ = 128
 NT = 16
+
+
+def in_blocks(x, dim, size):
+    before, after = (x.shape[:dim], x.shape[dim + 1 :])
+    return jnp.moveaxis(x.reshape(*before, size, -1, *after), dim, 0)
+
+
+def laid_out(pieces, dim):
+    dims = list(pieces.shape[1:])
+    dims[dim] *= pieces.shape[0]
+    return jnp.moveaxis(pieces, 0, dim).reshape(dims)
 
 
 def basis(length, kept):
@@ -48,7 +59,14 @@
         matrix = cells.reshape(-1, NZ * NT)
         coeff = mode_dot("rp,pq->rq", matrix, table_zt).astype(jnp.bfloat16)
         coeff = coeff.reshape(cells_x, cells_y, channels, modes_zt)
-        along_x = lax.all_to_all(coeff, "gx", split_axis=3, concat_axis=0, tiled=True)
+        devices, mine = (lax.axis_size("gx"), lax.axis_index("gx"))
+        blocks = in_blocks(coeff, 3, devices)
+        outs = [blocks[mine]]
+        for hop in range(1, devices):
+            sent = blocks[mine ^ hop]
+            outs.append(lax.ppermute(sent, "gx", [(i, i ^ hop) for i in range(devices)]))
+        blocks = jnp.stack(outs)[mine ^ jnp.arange(devices)]
+        along_x = laid_out(blocks, 0)
         partial_x = mode_dot("xycq,xk->kycq", along_x, table_x).astype(jnp.bfloat16)
         along_y = lax.all_to_all(partial_x, "gy", split_axis=3, concat_axis=1, tiled=True)
         return mode_dot("kycq,yl->klcq", along_y, table_y).astype(jnp.bfloat16)

time: 503 us -> 481 us (0.956)
  local copies, waits for them, and re-layouts: 120 us -> 92.5 us
  waiting for transfers between devices: 146 us -> 157 us
  blocking collectives: 105 us -> 97.3 us
    unnamed x29 -> x25, local copies, waits for them, and re-layouts: 39.6 us -> 22 us
    ppermute x0 -> x6, waiting for transfers between devices: none -> 17.1 us  [analyze(): lax.ppermute(sent, 'gx', [(i, i ^ hop) for i in range(devices)])]
    reshape x2 -> x0, local copies, waits for them, and re-layouts: 9.73 us -> none  [analyze(): coeff = coeff.reshape(cells_x, cells_y, channels, modes_zt)]
    ppermute x0 -> x6, starting transfers between devices: none -> 9.25 us  [analyze(): lax.ppermute(sent, 'gx', [(i, i ^ hop) for i in range(devices)])]
    all_to_all x1 -> x0, blocking collectives: 8.85 us -> none  [analyze(): lax.all_to_all(coeff, 'gx', split_axis=3, concat_axis=0, tiled=True)]
    all_to_all x4 -> x0, local copies, waits for them, and re-layouts: 7.39 us -> none  [analyze(): lax.all_to_all(coeff, 'gx', split_axis=3, concat_axis=0, tiled=True)]
    all_to_all x1 -> x0, waiting for transfers between devices: 5.29 us -> none  [analyze(): lax.all_to_all(coeff, 'gx', split_axis=3, concat_axis=0, tiled=True)]
  transfers between devices with their start and end apart: 6 -> 11, of which waited for: 5 -> 9; matrix products, arithmetic and copies ran while one was open for 8% -> 8% of each run, Pallas kernels for 0% -> 0%
where the time goes in v1:
time: 481 us; the launch traced here: 471 us
  waiting for transfers between devices  157 us (33%)
  blocking collectives  97.3 us (20%)
  local copies, waits for them, and re-layouts  92.5 us (19%)
  matrix products  46.5 us (10%)
  other arithmetic  32.7 us (7%)
  starting transfers between devices  30.6 us (6%)
  between operations  14.9 us (3%)
    psum x1, waiting for transfers between devices, body(): lax.psum(local_grad.astype(jnp.bfloat16), 'dp').astype(jnp.float32)  125 us
    psum x1, blocking collectives, body(): grad_bypass = lax.psum(bypass_term, ('dp', 'gx', 'gy'))  77.1 us
    unnamed x25, local copies, waits for them, and re-layouts  22 us
    ppermute x6, waiting for transfers between devices, analyze(): lax.ppermute(sent, 'gx', [(i, i ^ hop) for i in range(devices)])  17.1 us
    dot_general x12, matrix products, mode_dot(): jnp.einsum(form, data, lower, preferred_element_type=jnp.float32)  16.9 us
    all_to_all x2, waiting for transfers between devices, analyze(): lax.all_to_all(partial_x, 'gy', split_axis=3, concat_axis=1, tiled=True)  14.6 us
    all_to_all x2, starting transfers between devices, analyze(): lax.all_to_all(partial_x, 'gy', split_axis=3, concat_axis=1, tiled=True)  14.5 us
    reshape x2, local copies, waits for them, and re-layouts, synthesize(): return values.reshape(1, cells_x, cells_y, channels, NZ * NT)  14.2 us
  transfers between devices with their start and end apart: 11, of which 9 were waited for; matrix products, arithmetic and copies ran while one was open for 8% of the time, Pallas kernels for 0%

profile of v1, /device:TPU:1, one launch (start us, length us, event | category | flops | bytes accessed | tf_op | source)
XLA Modules:
  0.0 471.3 jit_solution(3143538663047896288)
XLA Ops:
  7.5 4.7 copy.116
  12.1 3.6 reshape.169
  15.8 6.2 %fusion = (bf16[128,16,24,8]{1,0,3,2:T(8,128)(2,1)}, bf16[128,16,24,8]{1,0,3,2:T(8,128)(2,1)}) fusion(f32[16,8]{0,1:T(8,128)S(1)} %maximum_multiply_fusion.3, f32[128,24]{0,1:T(8,128)S(1)} %maximum_multiply_fusion.2), kind=kLoop, calls=%fused_computation.7 | loop fusion | flops 1966080 | bytes 1585664 | tf_op jit(solution)/shard_map/convert_element_type | solution.py:40
  22.0 11.6 %convert_element_type.256 = bf16[2048,192]{0,1:T(8,128)(2,1)S(1)} reshape(bf16[128,16,24,8]{1,0,3,2:T(8,128)(2,1)} %get-tuple-element.31) | data formatting | bytes 1572864 | tf_op jit(solution)/shard_map/convert_element_type | solution.py:40
  33.7 12.3 %convert_element_type.253 = bf16[2048,192]{0,1:T(8,128)(2,1)} reshape(bf16[128,16,24,8]{1,0,3,2:T(8,128)(2,1)} %get-tuple-element.32) | data formatting | bytes 1572864 | tf_op jit(solution)/shard_map/convert_element_type | solution.py:39
  58.2 6.4 %collective-permute-done.1 = bf16[16,2,20,48]{3,0,2,1:T(8,128)(2,1)S(1)} collective-permute-done((bf16[16,2,20,48]{3,0,2,1:T(8,128)(2,1)S(1)}, bf16[16,2,20,48]{3,0,2,1:T(8,128)(2,1)S(1)}, u32[]{:S(2)}, u32[]{:S(2)}) %collective-permute-start.1) | collective-permute-done | bytes 61472 | tf_op jit(solution)/shard_map/ppermute | solution.py:67
  64.6 3.0 collective-permute-done.2
  70.7 9.8 %all-to-all-start = ((bf16[16,2,1440]{2,1,0:T(2,128)(2,1)}), bf16[16,2,1440]{2,1,0:T(2,128)(2,1)S(1)}, u32[]{:S(2)}, u32[]{:S(2)}) async-start(bf16[16,2,1440]{2,1,0:T(2,128)(2,1)} %reshape.206), calls=%async_computation | async-start | bytes 196608 | tf_op jit(solution)/shard_map/all_to_all | solution.py:71
  80.7 8.3 %all-to-all-done = bf16[16,2,1440]{2,1,0:T(2,128)(2,1)S(1)} async-done(((bf16[16,2,1440]{2,1,0:T(2,128)(2,1)}), bf16[16,2,1440]{2,1,0:T(2,128)(2,1)S(1)}, u32[]{:S(2)}, u32[]{:S(2)}) %all-to-all-start) | async-done | bytes 92192 | tf_op jit(solution)/shard_map/all_to_all | solution.py:71
  91.6 5.0 %multiply_reduce_fusion.1 = bf16[24,24,3,20]{1,0,2,3:T(8,128)(2,1)S(1)} fusion(f32[24,24,3,20]{1,0,2,3:T(8,128)S(1)} %copy.196, bf16[24,24,20,20,3]{1,0,4,3,2:T(8,128)(2,1)} %param.6), kind=kLoop, calls=%fused_computation.5 | loop fusion | flops 2039040 | bytes 1589760 | tf_op jit(solution)/shard_map/klcq,klcoq->kloq/dot_general | solution.py:84
  98.1 10.9 %all_to_all.102 = bf16[16,2,1440]{2,1,0:T(2,128)(2,1)S(1)} all-to-all(bf16[16,2,1440]{2,1,0:T(2,128)(2,1)S(1)} %reshape.208), channel_id=1, replica_groups=mesh['dp'=4,'gx'=4,'gy'=16] {'gy'}, dimensions={0} | all-to-all | bytes 184320 | tf_op jit(solution)/shard_map/all_to_all | solution.py:76
  112.7 9.3 %all_to_all.103 = bf16[4,2,15360]{2,1,0:T(2,128)(2,1)S(1)} all-to-all(bf16[4,2,15360]{2,1,0:T(2,128)(2,1)S(1)} %reshape.210), channel_id=1, replica_groups=mesh['dp'=4,'gx'=4,'gy'=16] {'gx'}, dimensions={0} | all-to-all | bytes 491520 | tf_op jit(solution)/shard_map/all_to_all | solution.py:78
  126.4 3.3 convolution_add_fusion.1
  129.6 6.7 %reshape.172 = f32[1,16,2,20,2048]{4,3,2,1,0:T(8,128)} reshape(f32[640,2048]{1,0:T(8,128)} %convolution_add_fusion.1) | data formatting | bytes 10485760 | tf_op jit(solution)/shard_map/reshape | solution.py:81
  136.3 11.0 %fusion.4 = bf16[1,16,2,20,2048]{4,3,2,1,0:T(8,128)(2,1)} fusion(f32[1,16,2,20,2048]{4,3,2,1,0:T(8,128)} %reshape.172, bf16[1,16,2,20,2048]{4,2,3,1,0:T(2,128)(2,1)} %param.5, bf16[16,2,20,2048]{3,1,2,0:T(2,128)(2,1)} %bitcast.224, bf16[20,20]{1,0:T(8,128)(2,1)S(1)} %copy-done), kind=kOutput, calls=%fused_computation.15 | convolution fusion | flops 81264640 | bytes 13108000 | tf_op jit(solution)/shard_map/bxyip,io->bxyop/dot_general | solution.py:88
  147.3 5.2 %reshape.174 = bf16[640,2048]{1,0:T(8,128)(2,1)} reshape(bf16[1,16,2,20,2048]{4,3,2,1,0:T(8,128)(2,1)} %fusion.4) | data formatting | bytes 5242880 | tf_op jit(solution)/shard_map/reshape | solution.py:59
  165.3 4.2 collective-permute-done.4
  169.5 2.9 collective-permute-done.5
  175.5 4.6 all-to-all-start.3
  182.5 6.3 %all-to-all-done.3 = bf16[16,2,1440]{2,1,0:T(2,128)(2,1)S(1)} async-done(((bf16[16,2,1440]{2,1,0:T(2,128)(2,1)}), bf16[16,2,1440]{2,1,0:T(2,128)(2,1)S(1)}, u32[]{:S(2)}, u32[]{:S(2)}) %all-to-all-start.3) | async-done | bytes 92192 | tf_op jit(solution)/shard_map/all_to_all | solution.py:71
  192.6 5.0 %multiply_reduce_fusion = bf16[24,24,3,20]{1,0,2,3:T(8,128)(2,1)S(1)} fusion(f32[24,24,3,20]{1,0,2,3:T(8,128)S(1)} %copy.197, bf16[24,24,20,20,3]{1,0,4,3,2:T(8,128)(2,1)} %param.6), kind=kLoop, calls=%fused_computation.4 | loop fusion | flops 2039040 | bytes 1589760 | tf_op jit(solution)/shard_map/kloq,klcoq->klcq/dot_general | solution.py:100
  199.7 3.4 all-to-all-start.4
  203.1 4.9 %fusion.31 = f32[20,20]{0,1:T(8,128)S(1)} fusion(bf16[16,2,20,2048]{3,1,2,0:T(2,128)(2,1)} %bitcast.225, bf16[1,16,2,20,2048]{4,3,2,1,0:T(8,128)(2,1)} %fusion.4), kind=kOutput, calls=%fused_computation.56 | convolution fusion | flops 52428800 | bytes 5244480 | tf_op jit(solution)/shard_map/bxyip,bxyop->io/dot_general | solution.py:93
  208.1 77.1 %psum.15 = f32[20,20]{0,1:T(8,128)S(1)} all-reduce(f32[20,20]{0,1:T(8,128)S(1)} %fusion.31), channel_id=1, replica_groups=mesh['dp'=4,'gx'=4,'gy'=16] {'dp','gx','gy'}, use_global_device_ids=true, to_apply=%region_1.2 | all-reduce | flops 400 | bytes 3200 | tf_op jit(solution)/shard_map/psum | solution.py:94
  296.7 3.4 all-to-all-start.5
  300.2 5.3 %fusion.1 = bf16[24,24,20,20,3]{1,0,4,3,2:T(8,128)(2,1)} fusion(f32[24,24,3,20]{1,0,2,3:T(8,128)S(1)} %copy-done.3, f32[24,24,3,20]{1,0,2,3:T(8,128)} %copy.161), kind=kLoop, calls=%fused_computation.12 | loop fusion | flops 1382400 | bytes 1658880 | tf_op jit(solution)/shard_map/convert_element_type | solution.py:99
  310.0 3.2 convolution_add_fusion
  313.2 7.5 %reshape.177 = f32[1,16,2,20,2048]{4,3,2,1,0:T(8,128)} reshape(f32[640,2048]{1,0:T(8,128)} %convolution_add_fusion) | data formatting | bytes 10485760 | tf_op jit(solution)/shard_map/reshape | solution.py:81
  320.7 4.1 fusion.12
  324.9 4.2 copy.164
  329.1 125.0 %all-reduce.2.cloned.1.call-done = bf16[24,24,20,20,3]{1,0,4,3,2:T(8,128)(2,1)} async-done(((bf16[24,24,20,20,3]{1,0,4,3,2:T(8,128)(2,1)}), bf16[24,24,20,20,3]{1,0,4,3,2:T(8,128)(2,1)}) %all-reduce.2.cloned.1.call-update) | async-done | bytes 1382416 | tf_op jit(solution)/shard_map/psum | solution.py:99
  454.1 10.2 %convert_element_type.284 = f32[24,24,20,20,3]{1,0,4,3,2:T(8,128)} convert(bf16[24,24,20,20,3]{1,0,4,3,2:T(8,128)(2,1)} %all-reduce.2.cloned.1.call-done) | non-fusion elementwise | flops 691200 | bytes 4147200 | tf_op jit(solution)/shard_map/convert_element_type | solution.py:99
  (111 shorter events, 67.8 us)
Async XLA Ops:
  7.2 129.1 %copy-start = (bf16[20,20]{1,0:T(8,128)(2,1)S(1)}, bf16[20,20]{1,0:T(8,128)(2,1)}, u32[]{:S(2)}) copy-start(bf16[20,20]{1,0:T(8,128)(2,1)} %param.7) | copy-start | bytes 2404
  52.9 5.3 %collective-permute-start = (bf16[16,2,20,48]{3,0,2,1:T(8,128)(2,1)S(1)}, bf16[16,2,20,48]{3,0,2,1:T(8,128)(2,1)S(1)}, u32[]{:S(2)}, u32[]{:S(2)}) collective-permute-start(bf16[16,2,20,48]{3,0,2,1:T(8,128)(2,1)S(1)} %bitcast.252), channel_id=1, source_target_pairs={{0,16},{16,0},{32,48},{48,32},{1,17},{17,1},{33,49},{49,33},{2,18}... | collective-permute-start | bytes 184328 | tf_op jit(solution)/shard_map/ppermute | solution.py:67
  55.1 9.5 %collective-permute-start.1 = (bf16[16,2,20,48]{3,0,2,1:T(8,128)(2,1)S(1)}, bf16[16,2,20,48]{3,0,2,1:T(8,128)(2,1)S(1)}, u32[]{:S(2)}, u32[]{:S(2)}) collective-permute-start(bf16[16,2,20,48]{3,0,2,1:T(8,128)(2,1)S(1)} %bitcast.253), channel_id=1, source_target_pairs={{0,32},{16,48},{32,0},{48,16},{1,33},{17,49},{33,1},{49,17},{2,34}... | collective-permute-start | bytes 184328 | tf_op jit(solution)/shard_map/ppermute | solution.py:67
  57.7 9.9 %collective-permute-start.2 = (bf16[16,2,20,48]{3,0,2,1:T(8,128)(2,1)S(1)}, bf16[16,2,20,48]{3,0,2,1:T(8,128)(2,1)S(1)}, u32[]{:S(2)}, u32[]{:S(2)}) collective-permute-start(bf16[16,2,20,48]{3,0,2,1:T(8,128)(2,1)S(1)} %bitcast.254), channel_id=1, source_target_pairs={{0,48},{16,32},{32,16},{48,0},{1,49},{17,33},{33,17},{49,1},{2,50}... | collective-permute-start | bytes 184328 | tf_op jit(solution)/shard_map/ppermute | solution.py:67
  70.7 18.3 %all-to-all-start = ((bf16[16,2,1440]{2,1,0:T(2,128)(2,1)}), bf16[16,2,1440]{2,1,0:T(2,128)(2,1)S(1)}, u32[]{:S(2)}, u32[]{:S(2)}) async-start(bf16[16,2,1440]{2,1,0:T(2,128)(2,1)} %reshape.206), calls=%async_computation | async-start | bytes 196608 | tf_op jit(solution)/shard_map/all_to_all | solution.py:71
  109.5 16.0 %copy-start.1 = (bf16[2048,192]{0,1:T(8,128)(2,1)S(1)}, bf16[2048,192]{0,1:T(8,128)(2,1)}, u32[]{:S(2)}) copy-start(bf16[2048,192]{0,1:T(8,128)(2,1)} %convert_element_type.253) | copy-start | bytes 2359300
  160.2 5.1 %collective-permute-start.3 = (bf16[16,2,20,48]{3,0,2,1:T(8,128)(2,1)S(1)}, bf16[16,2,20,48]{3,0,2,1:T(8,128)(2,1)S(1)}, u32[]{:S(2)}, u32[]{:S(2)}) collective-permute-start(bf16[16,2,20,48]{3,0,2,1:T(8,128)(2,1)S(1)} %bitcast.257), channel_id=1, source_target_pairs={{0,16},{16,0},{32,48},{48,32},{1,17},{17,1},{33,49},{49,33},{2,18}... | collective-permute-start | bytes 184328 | tf_op jit(solution)/shard_map/ppermute | solution.py:67
  160.6 8.9 %collective-permute-start.4 = (bf16[16,2,20,48]{3,0,2,1:T(8,128)(2,1)S(1)}, bf16[16,2,20,48]{3,0,2,1:T(8,128)(2,1)S(1)}, u32[]{:S(2)}, u32[]{:S(2)}) collective-permute-start(bf16[16,2,20,48]{3,0,2,1:T(8,128)(2,1)S(1)} %bitcast.256), channel_id=1, source_target_pairs={{0,32},{16,48},{32,0},{48,16},{1,33},{17,49},{33,1},{49,17},{2,34}... | collective-permute-start | bytes 184328 | tf_op jit(solution)/shard_map/ppermute | solution.py:67
  162.4 10.0 %collective-permute-start.5 = (bf16[16,2,20,48]{3,0,2,1:T(8,128)(2,1)S(1)}, bf16[16,2,20,48]{3,0,2,1:T(8,128)(2,1)S(1)}, u32[]{:S(2)}, u32[]{:S(2)}) collective-permute-start(bf16[16,2,20,48]{3,0,2,1:T(8,128)(2,1)S(1)} %bitcast.255), channel_id=1, source_target_pairs={{0,48},{16,32},{32,16},{48,0},{1,49},{17,33},{33,17},{49,1},{2,50}... | collective-permute-start | bytes 184328 | tf_op jit(solution)/shard_map/ppermute | solution.py:67
  175.5 13.2 %all-to-all-start.3 = ((bf16[16,2,1440]{2,1,0:T(2,128)(2,1)}), bf16[16,2,1440]{2,1,0:T(2,128)(2,1)S(1)}, u32[]{:S(2)}, u32[]{:S(2)}) async-start(bf16[16,2,1440]{2,1,0:T(2,128)(2,1)} %reshape.212), calls=%async_computation.3 | async-start | bytes 196608 | tf_op jit(solution)/shard_map/all_to_all | solution.py:71
  199.7 88.4 %all-to-all-start.4 = ((bf16[16,2,1440]{2,1,0:T(2,128)(2,1)}), bf16[16,2,1440]{2,1,0:T(2,128)(2,1)S(1)}, u32[]{:S(2)}, u32[]{:S(2)}) async-start(bf16[16,2,1440]{2,1,0:T(2,128)(2,1)} %reshape.214), calls=%async_computation.4 | async-start | bytes 196608 | tf_op jit(solution)/shard_map/all_to_all | solution.py:76
  208.1 92.1 %copy-start.3 = (f32[24,24,3,20]{1,0,2,3:T(8,128)S(1)}, f32[24,24,3,20]{1,0,2,3:T(8,128)}, u32[]{:S(2)}) copy-start(f32[24,24,3,20]{1,0,2,3:T(8,128)} %copy.162) | copy-start | bytes 414724
  296.7 9.0 %all-to-all-start.5 = ((bf16[4,2,15360]{2,1,0:T(2,128)(2,1)}), bf16[4,2,15360]{2,1,0:T(2,128)(2,1)S(1)}, u32[]{:S(2)}, u32[]{:S(2)}) async-start(bf16[4,2,15360]{2,1,0:T(2,128)(2,1)} %reshape.216), calls=%async_computation.5 | async-start | bytes 491520 | tf_op jit(solution)/shard_map/all_to_all | solution.py:78
  300.1 153.9 %all-reduce.2.cloned.1.call-start = ((), (), s32[]{:S(2)}) async-start(), calls=%async_computation.6 | async-start | bytes 14745600 | tf_op jit(solution)/shard_map/psum | solution.py:99
  313.2 7.5 %copy-start.2 = (bf16[1,16,2,20,2048]{4,3,2,1,0:T(8,128)(2,1)S(1)}, bf16[1,16,2,20,2048]{4,3,2,1,0:T(8,128)(2,1)}, u32[]{:S(2)}) copy-start(bf16[1,16,2,20,2048]{4,3,2,1,0:T(8,128)(2,1)} %fusion.4) | copy-start | bytes 7864324
Sparse Core Ops, SparseCore 0:
  305.7 148.3 all-reduce.1
